TPU v7x, 32 devices: a whole 2x2x4 slice. The times are simulated.
32 devices in a mesh: quad: 16 (over z, x, core), rows: 2 (over y).
Axes of the slice: x: 2, y: 2, z: 4, core: 2. Of those that a mesh axis runs over, the one named last changes fastest.
Arguments:
- solutions: bfloat16 [32, 2, 64, 16, 1280], P('quad', None, None, None, 'rows'), may hold values from -64 to 64
- angles: float32 [32], replicated, may hold values from -3.140625 to 3.140625
- qweights: float32 [2, 32], replicated, may hold values from -1 to 1
- neighbours: int32 [320, 8], P(('quad', 'rows')), may hold values from 0 to 319, as said below
- hblocks: bfloat16 [320, 64, 512], P(('quad', 'rows')), may hold values from -0.25 to 0.25
Outputs:
- h_moments: bfloat16 [1024, 20480], P(None, ('quad', 'rows'))
- ritz_matrices: float32 [512, 2, 2, 512], P('quad')
Inputs may be any that keep to these rules, and one draw needn't show every extreme that they name: neighbours[c, 0] = c, neighbours[c, 1] = min(c + 2, 319), neighbours[c, 2] = max(c - 2, 0); every entry lies within 2 of c.
All inputs are finite; a program needn't handle non-finite values.
Results may differ from a plain program's by a relative error of at most 0.0075.
Values may be sent and summed in bfloat16 or wider, within the bound.
A program may use at most 64 MiB of HBM per device.

v0:
```python
import jax
import jax.numpy as jnp
from jax import lax
from jax.sharding import PartitionSpec as P

LCOL = 64
QPTS = 32
KMOM = 8
NB = 8
HALO = 2


def extended(block, sides, width):
    for axis, dim in sides:
        count = lax.axis_size(axis)
        forward = [(i, i + 1) for i in range(count - 1)]
        backward = [(target, source) for source, target in forward]
        low = lax.ppermute(
            lax.slice_in_dim(block, block.shape[dim] - width, None, axis=dim), axis, forward
        )
        high = lax.ppermute(lax.slice_in_dim(block, 0, width, axis=dim), axis, backward)
        block = jnp.concatenate([low, block, high], axis=dim)
    return block


def moment_coefficients(angles, qweights):
    order = jnp.arange(KMOM, dtype=jnp.float32)[:, None]
    phase = order * angles[None, :]
    cosine = jnp.cos(phase)
    sine = jnp.sin(phase)
    real_coef = qweights[0][None, :] * cosine - qweights[1][None, :] * sine
    imag_coef = qweights[0][None, :] * sine + qweights[1][None, :] * cosine
    real_rows = jnp.stack([real_coef, -imag_coef], -1)
    imag_rows = jnp.stack([imag_coef, real_coef], -1)
    mixing = jnp.stack([real_rows, imag_rows], 0)
    return mixing.reshape(2 * KMOM, 2 * QPTS).astype(jnp.bfloat16)


def split_parts(product, half_cols, row_count):
    real_part = product[:row_count, :half_cols] + product[row_count:, half_cols:]
    imag_part = product[:row_count, half_cols:] - product[row_count:, :half_cols]
    return jnp.stack([real_part, imag_part], 1)


def gram_part(moments, applied, first_row, row_count, total_rows):
    half_cols = moments.shape[0] // 2
    chosen = jnp.concatenate(
        [
            lax.dynamic_slice_in_dim(moments, first_row, row_count, 0),
            lax.dynamic_slice_in_dim(moments, half_cols + first_row, row_count, 0),
        ],
        0,
    )
    contract = (((1,), (1,)), ((), ()))
    plain = lax.dot_general(chosen, moments, contract, preferred_element_type=jnp.float32)
    mixed = lax.dot_general(chosen, applied, contract, preferred_element_type=jnp.float32)
    ritz = jnp.stack(
        [split_parts(plain, half_cols, row_count), split_parts(mixed, half_cols, row_count)], 1
    )
    return ritz * (1.0 / total_rows)


def per_device(solutions, angles, qweights, neighbours, hblocks):
    groups = lax.axis_size("quad") * lax.axis_size("rows")
    rows_dev = solutions.shape[4]
    cells_dev = hblocks.shape[0]
    orbitals = hblocks.shape[1]
    half_cols = KMOM * LCOL
    mixing = moment_coefficients(angles, qweights)
    received = lax.all_to_all(solutions, "quad", split_axis=3, concat_axis=0, tiled=True)
    stacked = received.reshape(QPTS * 2, LCOL, received.shape[4])
    result = jnp.einsum("pq,qln->pln", mixing, stacked, preferred_element_type=jnp.float32)
    moments = result.reshape(2 * half_cols, received.shape[4]).astype(jnp.bfloat16)
    padded = extended(moments, ((("quad", "rows"), 1),), HALO * orbitals)
    first_cell = (
        lax.axis_index("quad") * lax.axis_size("rows") + lax.axis_index("rows")
    ) * cells_dev
    local_index = (neighbours - first_cell + HALO).reshape(-1)
    cellwise = padded.reshape(2 * half_cols, cells_dev + 2 * HALO, orbitals)
    nearby = jnp.take(cellwise, local_index, axis=1).reshape(
        2 * half_cols, cells_dev, NB * orbitals
    )
    applied = jnp.einsum("cam,xcm->xca", hblocks, nearby, preferred_element_type=jnp.float32)
    applied = applied.reshape(2 * half_cols, rows_dev).astype(jnp.bfloat16)
    total_rows = rows_dev * groups
    share_rows = half_cols // lax.axis_size("quad")
    summed = lax.psum(gram_part(moments, applied, 0, half_cols, total_rows), ("quad", "rows"))
    ritz_matrices = lax.dynamic_slice_in_dim(
        summed, lax.axis_index("quad") * share_rows, share_rows, 0
    )
    return (applied, ritz_matrices)


def solution(mesh):
    in_specs = (
        P("quad", None, None, None, "rows"),
        P(),
        P(),
        P(("quad", "rows"), None),
        P(("quad", "rows"), None, None),
    )
    out_specs = (P(None, ("quad", "rows")), P("quad", None, None, None))
    return jax.shard_map(
        per_device, mesh=mesh, in_specs=in_specs, out_specs=out_specs, check_vma=False
    )
```

profile of v0, /device:TPU:0, one launch (start us, length us, event | category | flops | bytes accessed | tf_op | source)
XLA Modules:
  0.0 333.4 jit_solution(11366127904357081607)
XLA Ops:
  7.2 0.0 copy-start
  7.2 6.2 %copy.34 = bf16[2,2,64,16,640]{4,2,1,0,3:T(8,128)(2,1)} copy(bf16[2,2,64,16,640]{4,3,2,1,0:T(8,128)(2,1)} %param.5) | data formatting | bytes 10485760 | tf_op args[0]
  13.3 0.0 copy-start.5
  13.3 0.0 copy-start.6
  13.3 0.0 copy-start.4
  13.3 7.5 %all-to-all-start = ((bf16[2,2,64,16,640]{4,2,1,0,3:T(8,128)(2,1)}), bf16[2,2,64,16,640]{4,2,1,0,3:T(8,128)(2,1)}, u32[]{:S(2)}, u32[]{:S(2)}) async-start(bf16[2,2,64,16,640]{4,2,1,0,3:T(8,128)(2,1)} %copy.34), calls=%async_computation | async-start | bytes 10485760 | tf_op jit(solution)/shard_map/all_to_all | solution.py:70
  20.9 0.0 all-reduce.2.cloned.1.call-start
  20.9 0.0 copy-done.5
  21.0 0.0 copy-done.6
  21.0 0.1 negate_convert_fusion
  21.0 0.1 copy.33
  21.2 0.1 convert_element_type.30
  21.3 0.0 copy-done.4
  21.3 0.1 copy.39
  21.4 0.1 reshape.334
  21.5 0.1 copy.32
  21.6 0.1 broadcast_in_dim.16
  21.6 0.1 broadcast_in_dim.17
  21.8 95.1 %all-to-all-done = bf16[2,2,64,16,640]{4,2,1,0,3:T(8,128)(2,1)} async-done(((bf16[2,2,64,16,640]{4,2,1,0,3:T(8,128)(2,1)}), bf16[2,2,64,16,640]{4,2,1,0,3:T(8,128)(2,1)}, u32[]{:S(2)}, u32[]{:S(2)}) %all-to-all-start) | async-done | bytes 5242912 | tf_op jit(solution)/shard_map/all_to_all | solution.py:70
  116.8 6.5 %fusion.6 = bf16[16,64,640]{2,0,1:T(8,128)(2,1)S(1)} fusion(bf16[64,64,640]{2,1,0:T(8,128)(2,1)} %bitcast.7, bf16[16,64]{0,1:T(8,128)(2,1)S(1)} %convert_element_type.30), kind=kOutput, calls=%fused_computation.11 | convolution fusion | flops 84541440 | bytes 6555648 | tf_op jit(solution)/shard_map/pq,qln->pln/dot_general | solution.py:72
  123.3 0.3 copy.37
  123.6 0.0 copy-start.1
  123.7 1.8 fusion.23
  125.5 3.4 %collective-permute-start = (bf16[1024,128]{1,0:T(8,128)(2,1)S(1)}, bf16[1024,128]{1,0:T(8,128)(2,1)S(1)}, u32[]{:S(2)}, u32[]{:S(2)}) collective-permute-start(bf16[1024,128]{1,0:T(8,128)(2,1)S(1)} %get-tuple-element.14), channel_id=1, source_target_pairs={{0,1},{1,2},{2,3},{3,4},{4,5},{5,6},{6,7},{7,8},{8,9},{9,10},{10,1... | collective-permute-start | bytes 786440 | tf_op jit(solution)/shard_map/ppermute | solution.py:18
  128.9 1.5 collective-permute-start.1
  130.4 1.5 fusion.15
  131.9 3.7 %collective-permute-done = bf16[1024,128]{1,0:T(8,128)(2,1)S(1)} collective-permute-done((bf16[1024,128]{1,0:T(8,128)(2,1)S(1)}, bf16[1024,128]{1,0:T(8,128)(2,1)S(1)}, u32[]{:S(2)}, u32[]{:S(2)}) %collective-permute-start) | collective-permute-done | bytes 262176 | tf_op jit(solution)/shard_map/ppermute | solution.py:18
  135.6 1.6 collective-permute-done.1
  137.2 0.0 copy-done.1
  137.2 1.4 pad_maximum_fusion
  138.6 2.9 copy.38
  141.5 6.3 %gather_fusion = bf16[80,1024,64]{1,2,0:T(8,128)(2,1)} fusion(bf16[1024,14,64]{0,2,1:T(8,128)(2,1)S(1)} %bitcast.45, s32[1024]{0:T(1024)S(1)} %pad_clamp_fusion), kind=kCustom, calls=%fused_computation | custom fusion | bytes 20971840 | tf_op jit(solution)/shard_map/jit(_take)/gather | solution.py:80
  147.8 0.0 copy-done
  147.8 0.0 copy-start.2
  147.8 5.5 %fusion.9 = bf16[10,1024,64]{1,2,0:T(8,128)(2,1)S(1)} fusion(bf16[10,64,512]{2,1,0:T(8,128)(2,1)S(1)} %copy-done, bf16[1024,10,512]{0,2,1:T(8,128)(2,1)} %bitcast.46, pred[10,512]{1,0:T(8,128)(4,1)S(1)} %broadcast_in_dim.17), kind=kOutput, calls=%fused_computation.12 | convolution fusion | flops 676986880 | bytes 12456960 | tf_op jit(solution)/shard_map/cam,xcm->xca/dot_general | solution.py:83
  153.4 0.0 copy-done.2
  153.4 1.8 fusion.24
  155.2 0.0 copy-start.3
  155.2 0.5 fusion.13
  155.7 0.7 copy-done.3
  156.4 0.4 maximum_bitcast_fusion
  156.9 2.7 maximum_multiply_fusion
  159.6 0.0 all-reduce.2.cloned.1.call-update
  159.6 1.4 copy.41
  161.1 163.6 %all-reduce.2.cloned.1.call-done = f32[512,2,2,512]{3,0,2,1:T(8,128)} async-done(((f32[512,2,2,512]{3,0,2,1:T(8,128)}), f32[512,2,2,512]{3,0,2,1:T(8,128)}) %all-reduce.2.cloned.1.call-update) | async-done | bytes 4194320 | tf_op jit(solution)/shard_map/psum | solution.py:87
  324.7 1.0 constant_dynamic-slice_fusion
  325.6 0.9 copy.42
  (8 shorter events, 0.1 us)
Async XLA Ops:
  7.2 140.7 %copy-start = (bf16[10,64,512]{2,1,0:T(8,128)(2,1)S(1)}, bf16[10,64,512]{2,1,0:T(8,128)(2,1)}, u32[]{:S(2)}) copy-start(bf16[10,64,512]{2,1,0:T(8,128)(2,1)} %param.9) | copy-start | bytes 1966084
  13.3 7.6 %copy-start.5 = (f32[2,32]{1,0:T(2,128)S(1)}, f32[2,32]{1,0:T(2,128)}, u32[]{:S(2)}) copy-start(f32[2,32]{1,0:T(2,128)} %param.7) | copy-start | bytes 772
  13.3 7.6 %copy-start.6 = (f32[32]{0:T(128)S(1)}, f32[32]{0:T(128)}, u32[]{:S(2)}) copy-start(f32[32]{0:T(128)} %param.6) | copy-start | bytes 388
  13.3 7.9 %copy-start.4 = (s32[10,8]{0,1:T(8,128)S(1)}, s32[10,8]{0,1:T(8,128)}, u32[]{:S(2)}) copy-start(s32[10,8]{0,1:T(8,128)} %param.8) | copy-start | bytes 964
  13.3 103.5 %all-to-all-start = ((bf16[2,2,64,16,640]{4,2,1,0,3:T(8,128)(2,1)}), bf16[2,2,64,16,640]{4,2,1,0,3:T(8,128)(2,1)}, u32[]{:S(2)}, u32[]{:S(2)}) async-start(bf16[2,2,64,16,640]{4,2,1,0,3:T(8,128)(2,1)} %copy.34), calls=%async_computation | async-start | bytes 10485760 | tf_op jit(solution)/shard_map/all_to_all | solution.py:70
  20.9 303.8 %all-reduce.2.cloned.1.call-start = ((), (), s32[]{:S(2)}) async-start(), calls=%async_computation.1 | async-start | bytes 8388608 | tf_op jit(solution)/shard_map/psum | solution.py:87
  123.6 13.6 %copy-start.1 = (bf16[16,64,640]{2,1,0:T(8,128)(2,1)}, bf16[16,64,640]{2,1,0:T(8,128)(2,1)S(1)}, u32[]{:S(2)}) copy-start(bf16[16,64,640]{2,1,0:T(8,128)(2,1)S(1)} %copy.37) | copy-start | bytes 3932164
  125.5 10.1 %collective-permute-start = (bf16[1024,128]{1,0:T(8,128)(2,1)S(1)}, bf16[1024,128]{1,0:T(8,128)(2,1)S(1)}, u32[]{:S(2)}, u32[]{:S(2)}) collective-permute-start(bf16[1024,128]{1,0:T(8,128)(2,1)S(1)} %get-tuple-element.14), channel_id=1, source_target_pairs={{0,1},{1,2},{2,3},{3,4},{4,5},{5,6},{6,7},{7,8},{8,9},{9,10},{10,1... | collective-permute-start | bytes 786440 | tf_op jit(solution)/shard_map/ppermute | solution.py:18
  128.9 8.3 %collective-permute-start.1 = (bf16[1024,128]{1,0:T(8,128)(2,1)S(1)}, bf16[1024,128]{1,0:T(8,128)(2,1)S(1)}, u32[]{:S(2)}, u32[]{:S(2)}) collective-permute-start(bf16[1024,128]{1,0:T(8,128)(2,1)S(1)} %get-tuple-element.15), channel_id=1, source_target_pairs={{1,0},{2,1},{3,2},{4,3},{5,4},{6,5},{7,6},{8,7},{9,8},{10,9},{11,1... | collective-permute-start | bytes 786440 | tf_op jit(solution)/shard_map/ppermute | solution.py:21
  147.8 5.6 %copy-start.2 = (bf16[16,64,640]{2,1,0:T(8,128)(2,1)S(1)}, bf16[16,64,640]{2,1,0:T(8,128)(2,1)}, u32[]{:S(2)}) copy-start(bf16[16,64,640]{2,1,0:T(8,128)(2,1)} %copy-done.1) | copy-start | bytes 3932164
  155.2 1.2 copy-start.3
Sparse Core Ops, SparseCore 0:
  159.7 164.8 all-reduce.1
where the time goes:
time: 334 us; the launch traced here: 333 us
  waiting for transfers between devices  264 us (79%)
  local copies, waits for them, and re-layouts  20.4 us (6%)
  matrix products  15.7 us (5%)
  between operations  14.2 us (4%)
  starting transfers between devices  12.5 us (4%)
  other arithmetic  6.65 us (2%)
    psum x1, waiting for transfers between devices, per_device(): lax.psum(gram_part(moments, applied, 0, half_cols, total_rows), ('quad',...  164 us
    all_to_all x1, waiting for transfers between devices, per_device(): lax.all_to_all(solutions, 'quad', split_axis=3, concat_axis=0, tiled=True)  95.1 us
    unnamed x17, local copies, waits for them, and re-layouts  9.26 us
    all_to_all x1, starting transfers between devices, per_device(): lax.all_to_all(solutions, 'quad', split_axis=3, concat_axis=0, tiled=True)  7.53 us
  transfers between devices with their start and end apart: 4, of which 4 were waited for; matrix products, arithmetic and copies ran while one was open for 1% of the time, Pallas kernels for 0%

commit v1 on v0

--- a/solution.py
+++ b/solution.py
@@ -67,7 +67,12 @@
     orbitals = hblocks.shape[1]
     half_cols = KMOM * LCOL
     mixing = moment_coefficients(angles, qweights)
-    received = lax.all_to_all(solutions, "quad", split_axis=3, concat_axis=0, tiled=True)
+    received = jnp.concatenate(
+        lax.all_to_all(
+            jnp.stack(jnp.split(solutions, lax.axis_size("quad"), axis=3)), "quad", 0, 0
+        ),
+        axis=0,
+    )
     stacked = received.reshape(QPTS * 2, LCOL, received.shape[4])
     result = jnp.einsum("pq,qln->pln", mixing, stacked, preferred_element_type=jnp.float32)
     moments = result.reshape(2 * half_cols, received.shape[4]).astype(jnp.bfloat16)

time: 334 us -> 362 us (1.084)
  local copies, waits for them, and re-layouts: 20.4 us -> 48.1 us
    split x0 -> x1, local copies, waits for them, and re-layouts: none -> 21.4 us  [per_device(): jnp.split(solutions, lax.axis_size('quad'), axis=3)]
    unnamed x17 -> x31, local copies, waits for them, and re-layouts: 9.26 us -> 14.8 us
where the time goes in v1:
time: 362 us; the launch traced here: 361 us
  waiting for transfers between devices  264 us (73%)
  local copies, waits for them, and re-layouts  48.1 us (13%)
  matrix products  15.7 us (4%)
  between operations  14.3 us (4%)
  starting transfers between devices  12.5 us (3%)
  other arithmetic  6.63 us (2%)
    psum x1, waiting for transfers between devices, per_device(): lax.psum(gram_part(moments, applied, 0, half_cols, total_rows), ('quad',...  164 us
    all_to_all x1, waiting for transfers between devices, per_device(): lax.all_to_all(jnp.stack(jnp.split(solutions, lax.axis_size('quad'), axis...  95.1 us
    split x1, local copies, waits for them, and re-layouts, per_device(): jnp.split(solutions, lax.axis_size('quad'), axis=3)  21.4 us
    unnamed x31, local copies, waits for them, and re-layouts  14.8 us
    all_to_all x1, starting transfers between devices, per_device(): lax.all_to_all(jnp.stack(jnp.split(solutions, lax.axis_size('quad'), axis...  7.53 us
  transfers between devices with their start and end apart: 4, of which 4 were waited for; matrix products, arithmetic and copies ran while one was open for 1% of the time, Pallas kernels for 0%

profile of v1, /device:TPU:0, one launch (start us, length us, event | category | flops | bytes accessed | tf_op | source)
XLA Modules:
  0.0 361.1 jit_solution(4098353681570204009)
XLA Ops:
  7.2 21.4 %fusion.38 = (bf16[2,2,64,1,640]{4,3,2,1,0:T(2,128)(2,1)S(1)}, bf16[2,2,64,1,640]{4,3,2,1,0:T(2,128)(2,1)S(1)}, bf16[2,2,64,1,640]{4,3,2,1,0:T(2,128)(2,1)S(1)},...) fusion(bf16[2,2,64,16,640]{4,3,2,1,0:T(8,128)(2,1)} %param.5), kind=kLoop, calls=%fused_computation.74 | loop fusion | bytes 10485760 | tf_op jit(solution)/shard_map/split | solution.py:72
  28.6 0.8 fusion.31
  29.4 0.8 fusion.30
  30.2 0.8 fusion.29
  30.9 0.8 fusion.28
  31.7 0.8 fusion.27
  32.5 0.8 fusion.26
  33.3 0.8 fusion.25
  34.0 0.8 fusion.24
  34.8 0.8 fusion.23
  35.6 0.8 fusion.22
  36.4 0.8 fusion.21
  37.2 0.8 fusion.20
  38.0 0.8 fusion.19
  38.8 0.8 fusion.18
  39.5 0.8 fusion.17
  40.3 0.8 fusion.16
  41.1 7.5 %all-to-all-start = ((bf16[16,2,2,64,1,640]{5,3,2,1,4,0:T(8,128)(2,1)}), bf16[16,2,2,64,1,640]{5,3,2,1,4,0:T(8,128)(2,1)}, u32[]{:S(2)}, u32[]{:S(2)}) async-start(bf16[16,2,2,64,1,640]{5,3,2,1,4,0:T(8,128)(2,1)} %fusion.16), calls=%async_computation | async-start | bytes 10485760 | tf_op jit(solution)/shard_map/all_to_all | solution.py:71
  48.7 0.1 negate_convert_fusion
  48.8 0.1 copy.54
  48.9 0.1 convert_element_type.30
  49.0 0.1 copy.75
  49.1 0.1 reshape.329
  49.2 0.1 copy.53
  49.3 0.1 broadcast_in_dim.16
  49.4 0.1 broadcast_in_dim.17
  49.5 95.1 %all-to-all-done = bf16[16,2,2,64,1,640]{5,3,2,1,4,0:T(8,128)(2,1)} async-done(((bf16[16,2,2,64,1,640]{5,3,2,1,4,0:T(8,128)(2,1)}), bf16[16,2,2,64,1,640]{5,3,2,1,4,0:T(8,128)(2,1)}, u32[]{:S(2)}, u32[]{:S(2)}) %all-to-all-start) | async-done | bytes 5242912 | tf_op jit(solution)/shard_map/all_to_all | solution.py:71
  144.6 6.5 %fusion.6 = bf16[16,64,640]{2,0,1:T(8,128)(2,1)S(1)} fusion(bf16[64,64,640]{2,1,0:T(8,128)(2,1)} %bitcast.21, bf16[16,64]{0,1:T(8,128)(2,1)S(1)} %convert_element_type.30), kind=kOutput, calls=%fused_computation.11 | convolution fusion | flops 84541440 | bytes 6555648 | tf_op jit(solution)/shard_map/pq,qln->pln/dot_general | solution.py:77
  151.1 0.3 copy.73
  151.4 1.8 fusion.40
  153.2 3.4 collective-permute-start
  156.7 1.5 collective-permute-start.1
  158.2 1.5 fusion.15
  159.6 3.7 %collective-permute-done = bf16[1024,128]{1,0:T(8,128)(2,1)S(1)} collective-permute-done((bf16[1024,128]{1,0:T(8,128)(2,1)S(1)}, bf16[1024,128]{1,0:T(8,128)(2,1)S(1)}, u32[]{:S(2)}, u32[]{:S(2)}) %collective-permute-start) | collective-permute-done | bytes 262176 | tf_op jit(solution)/shard_map/ppermute | solution.py:18
  163.4 1.6 collective-permute-done.1
  165.0 1.4 pad_maximum_fusion
  166.4 2.9 copy.74
  169.3 6.3 %gather_fusion = bf16[80,1024,64]{1,2,0:T(8,128)(2,1)} fusion(bf16[1024,14,64]{0,2,1:T(8,128)(2,1)S(1)} %bitcast.105, s32[1024]{0:T(1024)S(1)} %pad_clamp_fusion), kind=kCustom, calls=%fused_computation | custom fusion | bytes 20971840 | tf_op jit(solution)/shard_map/jit(_take)/gather | solution.py:85
  175.6 5.5 %fusion.9 = bf16[10,1024,64]{1,2,0:T(8,128)(2,1)S(1)} fusion(bf16[10,64,512]{2,1,0:T(8,128)(2,1)S(1)} %copy-done, bf16[1024,10,512]{0,2,1:T(8,128)(2,1)} %bitcast.106, pred[10,512]{1,0:T(8,128)(4,1)S(1)} %broadcast_in_dim.17), kind=kOutput, calls=%fused_computation.12 | convolution fusion | flops 676986880 | bytes 12456960 | tf_op jit(solution)/shard_map/cam,xcm->xca/dot_general | solution.py:88
  181.1 1.8 fusion.41
  182.9 0.5 fusion.13
  183.4 0.7 copy-done.3
  184.2 0.4 maximum_bitcast_fusion
  184.6 2.7 maximum_multiply_fusion
  187.4 1.4 copy.77
  188.8 163.6 %all-reduce.2.cloned.1.call-done = f32[512,2,2,512]{3,0,2,1:T(8,128)} async-done(((f32[512,2,2,512]{3,0,2,1:T(8,128)}), f32[512,2,2,512]{3,0,2,1:T(8,128)}) %all-reduce.2.cloned.1.call-update) | async-done | bytes 4194320 | tf_op jit(solution)/shard_map/psum | solution.py:92
  352.4 1.0 constant_dynamic-slice_fusion
  353.4 0.9 copy.78
  (23 shorter events, 0.2 us)
Async XLA Ops:
  7.2 168.4 %copy-start = (bf16[10,64,512]{2,1,0:T(8,128)(2,1)S(1)}, bf16[10,64,512]{2,1,0:T(8,128)(2,1)}, u32[]{:S(2)}) copy-start(bf16[10,64,512]{2,1,0:T(8,128)(2,1)} %param.9) | copy-start | bytes 1966084
  41.1 7.6 %copy-start.5 = (f32[2,32]{1,0:T(2,128)S(1)}, f32[2,32]{1,0:T(2,128)}, u32[]{:S(2)}) copy-start(f32[2,32]{1,0:T(2,128)} %param.7) | copy-start | bytes 772
  41.1 7.6 %copy-start.6 = (f32[32]{0:T(128)S(1)}, f32[32]{0:T(128)}, u32[]{:S(2)}) copy-start(f32[32]{0:T(128)} %param.6) | copy-start | bytes 388
  41.1 7.9 %copy-start.4 = (s32[10,8]{0,1:T(8,128)S(1)}, s32[10,8]{0,1:T(8,128)}, u32[]{:S(2)}) copy-start(s32[10,8]{0,1:T(8,128)} %param.8) | copy-start | bytes 964
  41.1 103.5 %all-to-all-start = ((bf16[16,2,2,64,1,640]{5,3,2,1,4,0:T(8,128)(2,1)}), bf16[16,2,2,64,1,640]{5,3,2,1,4,0:T(8,128)(2,1)}, u32[]{:S(2)}, u32[]{:S(2)}) async-start(bf16[16,2,2,64,1,640]{5,3,2,1,4,0:T(8,128)(2,1)} %fusion.16), calls=%async_computation | async-start | bytes 10485760 | tf_op jit(solution)/shard_map/all_to_all | solution.py:71
  48.6 303.8 %all-reduce.2.cloned.1.call-start = ((), (), s32[]{:S(2)}) async-start(), calls=%async_computation.1 | async-start | bytes 8388608 | tf_op jit(solution)/shard_map/psum | solution.py:92
  151.4 13.6 %copy-start.1 = (bf16[16,64,640]{2,1,0:T(8,128)(2,1)}, bf16[16,64,640]{2,1,0:T(8,128)(2,1)S(1)}, u32[]{:S(2)}) copy-start(bf16[16,64,640]{2,1,0:T(8,128)(2,1)S(1)} %copy.73) | copy-start | bytes 3932164
  153.2 10.1 %collective-permute-start = (bf16[1024,128]{1,0:T(8,128)(2,1)S(1)}, bf16[1024,128]{1,0:T(8,128)(2,1)S(1)}, u32[]{:S(2)}, u32[]{:S(2)}) collective-permute-start(bf16[1024,128]{1,0:T(8,128)(2,1)S(1)} %get-tuple-element.28), channel_id=1, source_target_pairs={{0,1},{1,2},{2,3},{3,4},{4,5},{5,6},{6,7},{7,8},{8,9},{9,10},{10,1... | collective-permute-start | bytes 786440 | tf_op jit(solution)/shard_map/ppermute | solution.py:18
  156.7 8.3 %collective-permute-start.1 = (bf16[1024,128]{1,0:T(8,128)(2,1)S(1)}, bf16[1024,128]{1,0:T(8,128)(2,1)S(1)}, u32[]{:S(2)}, u32[]{:S(2)}) collective-permute-start(bf16[1024,128]{1,0:T(8,128)(2,1)S(1)} %get-tuple-element.29), channel_id=1, source_target_pairs={{1,0},{2,1},{3,2},{4,3},{5,4},{6,5},{7,6},{8,7},{9,8},{10,9},{11,1... | collective-permute-start | bytes 786440 | tf_op jit(solution)/shard_map/ppermute | solution.py:21
  175.6 5.5 %copy-start.2 = (bf16[16,64,640]{2,1,0:T(8,128)(2,1)S(1)}, bf16[16,64,640]{2,1,0:T(8,128)(2,1)}, u32[]{:S(2)}) copy-start(bf16[16,64,640]{2,1,0:T(8,128)(2,1)} %copy-done.1) | copy-start | bytes 3932164
  182.9 1.2 copy-start.3
Sparse Core Ops, SparseCore 0:
  187.5 164.8 all-reduce.1
